TPU v7x, 32 devices: a whole 2x2x4 slice. The times are simulated.
32 devices in a mesh: row: 8 (over y, x, core), col: 4 (over z).
Axes of the slice: x: 2, y: 2, z: 4, core: 2. Of those that a mesh axis runs over, the one named last changes fastest.
Arguments:
- sensitivity: bfloat16 [512, 24576], P(('row', 'col')), may hold values from -0.25 to 0.25
- sensor_of_row: int32 [512], P(('row', 'col')), may hold values from 0 to 127
- row_class: int32 [512], P(('row', 'col')), may hold values from 0 to 3
- sensor_precision: float32 [128], replicated, may hold values from 0.25 to 4
- class_weight: float32 [4], replicated, may hold values from 0.25 to 2.5
Outputs:
- hessian: float32 [4, 24576, 6144], P('col', 'row')
All inputs are finite; a program needn't handle non-finite values.
Results may differ from a plain program's by a relative error of at most 0.004.
Values may be sent and summed in bfloat16 or wider, within the bound.
A program may use at most 192 MiB of HBM per device.

v0:
```python
import jax
import jax.numpy as jnp
from jax import lax
from jax.sharding import PartitionSpec as P


def contract(left, right):
    return lax.dot_general(
        left, right, (((0,), (0,)), ((), ())), preferred_element_type=jnp.float32
    )


def shards(sensitivity, sensor_of_row, row_class, sensor_precision, class_weight):
    row_count = lax.axis_size("row")
    col_count = lax.axis_size("col")
    width = sensitivity.shape[1]
    tile_width = width // row_count
    piece_width = tile_width // col_count
    col_index = lax.axis_index("col")
    sensor_match = (
        sensor_of_row[:, None] == jnp.arange(sensor_precision.shape[0], dtype=jnp.int32)[None, :]
    )
    class_match = row_class[:, None] == jnp.arange(class_weight.shape[0], dtype=jnp.int32)[None, :]
    precision = jnp.sum(jnp.where(sensor_match, sensor_precision[None, :], 0.0), axis=1)
    quality = jnp.sum(jnp.where(class_match, class_weight[None, :], 0.0), axis=1)
    scaled = (jnp.sqrt(precision * quality)[:, None] * sensitivity.astype(jnp.float32)).astype(
        jnp.bfloat16
    )
    pieces = lax.all_to_all(scaled, ("row", "col"), split_axis=1, concat_axis=0, tiled=True)
    own_tile = lax.all_gather(pieces, "col", axis=1, tiled=True)
    my_piece = lax.dynamic_slice_in_dim(own_tile, col_index * piece_width, piece_width, 1)
    block = contract(own_tile, lax.all_gather(my_piece, "row", axis=1, tiled=True))
    return block[None]


def solution(mesh):
    return jax.shard_map(
        shards,
        mesh=mesh,
        in_specs=(P(("row", "col"), None), P(("row", "col")), P(("row", "col")), P(), P()),
        out_specs=P("col", "row", None),
        check_vma=False,
    )
```

profile of v0, /device:TPU:0, one launch (start us, length us, event | category | flops | bytes accessed | tf_op | source)
XLA Modules:
  0.0 187.6 jit_solution(11318577829438510996)
XLA Ops:
  6.5 0.0 all-gather.3.cloned.1.call-start
  6.5 0.9 select_reduce_fusion
  7.4 0.8 select_reduce_fusion.1
  8.2 1.3 multiply_convert_fusion
  9.5 0.1 copy.11
  9.6 26.8 %all_to_all.19 = bf16[16,32,768]{2,0,1:T(8,128)(2,1)} all-to-all(bf16[16,32,768]{2,0,1:T(8,128)(2,1)S(1)} %bitcast.13), channel_id=1, replica_groups=mesh['row'=8,'col'=4] {'row','col'}, dimensions={1} | all-to-all | bytes 1572864 | tf_op jit(solution)/shard_map/all_to_all | solution.py:29
  36.4 0.0 all-gather.3.cloned.1.call-update
  36.4 0.0 all-gather.5.cloned.1.call-start
  36.5 63.3 %all-gather.3.cloned.1.call-done = bf16[512,3072]{1,0:T(8,128)(2,1)} async-done(((bf16[512,768]{1,0:T(8,128)(2,1)}), bf16[512,3072]{1,0:T(8,128)(2,1)}) %all-gather.3.cloned.1.call-update) | async-done | bytes 3145744 | tf_op jit(solution)/shard_map/all_gather | solution.py:30
  99.8 2.1 %constant_dynamic-slice_fusion = bf16[512,768]{1,0:T(8,128)(2,1)} fusion(bf16[512,3072]{1,0:T(8,128)(2,1)} %all-gather.3.cloned.1.call-done, s32[]{:T(128)S(6)} %select_n.13), kind=kLoop, calls=%fused_computation.8 | loop fusion | bytes 1572868 | tf_op jit(solution)/shard_map/dynamic_slice | solution.py:31
  101.9 0.0 all-gather.5.cloned.1.call-update
  101.9 44.2 %all-gather.5.cloned.1.call-done = bf16[512,6144]{1,0:T(8,128)(2,1)} async-done(((bf16[512,768]{1,0:T(8,128)(2,1)}), bf16[512,6144]{1,0:T(8,128)(2,1)}) %all-gather.5.cloned.1.call-update) | async-done | bytes 6291472 | tf_op jit(solution)/shard_map/all_gather | solution.py:32
  146.1 34.6 %convolution_bitcast_fusion = f32[1,3072,6144]{2,1,0:T(8,128)} fusion(bf16[512,3072]{1,0:T(8,128)(2,1)} %all-gather.3.cloned.1.call-done, bf16[512,6144]{1,0:T(8,128)(2,1)} %all-gather.5.cloned.1.call-done), kind=kOutput, calls=%fused_computation | convolution fusion | flops 19327352832 | bytes 84934656 | tf_op jit(solution)/shard_map/dot_general | solution.py:8
  (1 shorter events, 0.0 us)
Async XLA Ops:
  6.5 93.3 %all-gather.3.cloned.1.call-start = ((), (), s32[]{:S(2)}) async-start(), calls=%async_computation.1 | async-start | bytes 3932160 | tf_op jit(solution)/shard_map/all_gather | solution.py:30
  36.4 109.7 %all-gather.5.cloned.1.call-start = ((), (), s32[]{:S(2)}) async-start(), calls=%async_computation.2 | async-start | bytes 7077888 | tf_op jit(solution)/shard_map/all_gather | solution.py:32
Sparse Core Ops, SparseCore 0:
  36.5 63.2 all-gather.2
  102.0 44.0 all-gather.4
where the time goes:
time: 188 us
  waiting for transfers between devices  108 us (57%)
  matrix products  34.6 us (18%)
  blocking collectives  26.8 us (14%)
  between operations  13.4 us (7%)
  other arithmetic  2.95 us (2%)
  local copies, waits for them, and re-layouts  2.11 us (1%)
    all_gather x1, waiting for transfers between devices, shards(): own_tile = lax.all_gather(pieces, 'col', axis=1, tiled=True)  63.3 us
    all_gather x1, waiting for transfers between devices, shards(): lax.all_gather(my_piece, 'row', axis=1, tiled=True)  44.2 us
    dot_general x1, matrix products, contract(): lax.dot_general(left, right, (((0,), (0,)), ((), ())), preferred_element_...  34.6 us
    all_to_all x1, blocking collectives, shards(): lax.all_to_all(scaled, ('row', 'col'), split_axis=1, concat_axis=0, tiled...  26.8 us
  transfers between devices with their start and end apart: 2, of which 2 were waited for; matrix products, arithmetic and copies ran while one was open for 0% of the time, Pallas kernels for 0%

commit v1 on v0

--- a/solution.py
+++ b/solution.py
@@ -26,7 +26,15 @@
     scaled = (jnp.sqrt(precision * quality)[:, None] * sensitivity.astype(jnp.float32)).astype(
         jnp.bfloat16
     )
-    pieces = lax.all_to_all(scaled, ("row", "col"), split_axis=1, concat_axis=0, tiled=True)
+    pieces = jnp.concatenate(
+        lax.all_to_all(
+            jnp.stack(jnp.split(scaled, lax.axis_size(("row", "col")), axis=1)),
+            ("row", "col"),
+            0,
+            0,
+        ),
+        axis=0,
+    )
     own_tile = lax.all_gather(pieces, "col", axis=1, tiled=True)
     my_piece = lax.dynamic_slice_in_dim(own_tile, col_index * piece_width, piece_width, 1)
     block = contract(own_tile, lax.all_gather(my_piece, "row", axis=1, tiled=True))

time: 188 us -> 188 us (level)
  no operation moved by 1% of the time
where the time goes in v1:
time: 188 us
  waiting for transfers between devices  108 us (57%)
  matrix products  34.7 us (18%)
  blocking collectives  26.8 us (14%)
  between operations  13.7 us (7%)
  other arithmetic  2.95 us (2%)
  local copies, waits for them, and re-layouts  2.2 us (1%)
    all_gather x1, waiting for transfers between devices, shards(): own_tile = lax.all_gather(pieces, 'col', axis=1, tiled=True)  63.3 us
    all_gather x1, waiting for transfers between devices, shards(): lax.all_gather(my_piece, 'row', axis=1, tiled=True)  44.2 us
    dot_general x1, matrix products, contract(): lax.dot_general(left, right, (((0,), (0,)), ((), ())), preferred_element_...  34.7 us
    all_to_all x1, blocking collectives, shards(): lax.all_to_all(jnp.stack(jnp.split(scaled, lax.axis_size(('row', 'col')),...  26.8 us
  transfers between devices with their start and end apart: 2, of which 2 were waited for; matrix products, arithmetic and copies ran while one was open for 0% of the time, Pallas kernels for 0%

profile of v1, /device:TPU:0, one launch (start us, length us, event | category | flops | bytes accessed | tf_op | source)
XLA Modules:
  0.0 187.9 jit_solution(5868822057229475340)
XLA Ops:
  6.5 0.0 all-gather.3.cloned.1.call-start
  6.5 0.9 select_reduce_fusion
  7.4 0.8 select_reduce_fusion.1
  8.2 1.3 multiply_convert_fusion
  9.9 26.8 %all_to_all.5 = bf16[32,16,768]{2,1,0:T(8,128)(2,1)} all-to-all(bf16[32,16,768]{2,1,0:T(8,128)(2,1)S(1)} %constant_dynamic-update-slice_fusion), channel_id=1, replica_groups=mesh['row'=8,'col'=4] {'row','col'}, dimensions={0} | all-to-all | bytes 1572864 | tf_op jit(solution)/shard_map/all_to_all | solution.py:30
  36.7 0.0 all-gather.3.cloned.1.call-update
  36.7 0.0 all-gather.5.cloned.1.call-start
  36.8 63.3 %all-gather.3.cloned.1.call-done = bf16[512,3072]{1,0:T(8,128)(2,1)} async-done(((bf16[512,768]{1,0:T(8,128)(2,1)}), bf16[512,3072]{1,0:T(8,128)(2,1)}) %all-gather.3.cloned.1.call-update) | async-done | bytes 3145744 | tf_op jit(solution)/shard_map/all_gather | solution.py:38
  100.1 2.1 %constant_dynamic-slice_fusion = bf16[512,768]{1,0:T(8,128)(2,1)} fusion(bf16[512,3072]{1,0:T(8,128)(2,1)} %all-gather.3.cloned.1.call-done, s32[]{:T(128)S(6)} %select_n.13), kind=kLoop, calls=%fused_computation.71 | loop fusion | bytes 1572868 | tf_op jit(solution)/shard_map/dynamic_slice | solution.py:39
  102.2 0.0 all-gather.5.cloned.1.call-update
  102.2 44.2 %all-gather.5.cloned.1.call-done = bf16[512,6144]{1,0:T(8,128)(2,1)} async-done(((bf16[512,768]{1,0:T(8,128)(2,1)}), bf16[512,6144]{1,0:T(8,128)(2,1)}) %all-gather.5.cloned.1.call-update) | async-done | bytes 6291472 | tf_op jit(solution)/shard_map/all_gather | solution.py:40
  146.4 34.7 %convolution_bitcast_fusion = f32[1,3072,6144]{2,1,0:T(8,128)} fusion(bf16[512,3072]{1,0:T(8,128)(2,1)} %all-gather.3.cloned.1.call-done, bf16[512,6144]{1,0:T(8,128)(2,1)} %all-gather.5.cloned.1.call-done), kind=kOutput, calls=%fused_computation | convolution fusion | flops 19327352832 | bytes 84934656 | tf_op jit(solution)/shard_map/dot_general | solution.py:8
  (33 shorter events, 0.1 us)
Async XLA Ops:
  6.5 93.6 %all-gather.3.cloned.1.call-start = ((), (), s32[]{:S(2)}) async-start(), calls=%async_computation.1 | async-start | bytes 3932160 | tf_op jit(solution)/shard_map/all_gather | solution.py:38
  36.7 109.7 %all-gather.5.cloned.1.call-start = ((), (), s32[]{:S(2)}) async-start(), calls=%async_computation.2 | async-start | bytes 7077888 | tf_op jit(solution)/shard_map/all_gather | solution.py:40
Sparse Core Ops, SparseCore 0:
  36.9 63.2 all-gather.2
  102.3 44.0 all-gather.4
